TPU v7x, 256 devices: a whole 4x4x8 slice. The times are simulated.
256 devices in a mesh: seq: 64 (over y, z, core), tp: 4 (over x).
Axes of the slice: x: 4, y: 4, z: 8, core: 2. Of those that a mesh axis runs over, the one named last changes fastest.
Arguments:
- queries: bfloat16 [65536, 2048], P('seq', 'tp'), may hold values from -2 to 2
- keys: bfloat16 [65536, 2048], P('seq', 'tp'), may hold values from -2 to 2
- values: bfloat16 [65536, 2048], P('seq', 'tp'), may hold values from -16 to 16
- out_grad: bfloat16 [65536, 2048], P('seq', 'tp'), may hold values from -1.5 to 1.5
- gain: float32 [2048], P('tp'), may hold values from 0.25 to 1.75
Outputs:
- query_grad: bfloat16 [65536, 2048], P('seq', 'tp')
- key_grad: bfloat16 [65536, 2048], P('seq', 'tp')
- value_grad: bfloat16 [65536, 2048], P('seq', 'tp')
- gain_grad: float32 [2048], P('tp')
All inputs are finite; a program needn't handle non-finite values.
Results may differ from a plain program's by a relative error of at most 0.006.
Values sent between devices are 32-bit elements; how exact they have to be, the bound alone decides.
A program may use at most 128 MiB of HBM per device.

v0:
```python
import jax
import jax.numpy as jnp
from jax import lax
from jax.sharding import PartitionSpec as P

HEADS = 16
HEAD_DIM = 128
BLK = 512


epsilon = 1e-05


def entering(array, axis, combine, identity):
    peers, position = (lax.axis_size(axis), lax.axis_index(axis))
    everything = lax.all_gather(array, axis)
    start = jnp.broadcast_to(jnp.asarray(identity, array.dtype), array.shape)

    def step(k, before):
        at = peers - 1 - k
        reached = at > position
        new = combine(before, everything[at])
        return jnp.where(reached, new, before)

    return lax.fori_loop(0, peers, step, start)


def add_states(earlier, later):
    return earlier + later


def local(queries, keys, values, out_grad, gain):
    f32 = jnp.float32
    tok_rows = queries.shape[0]
    head_count = queries.shape[1] // HEAD_DIM
    block_count = tok_rows // BLK

    def block_view(array):
        return array.reshape(block_count, BLK, head_count, HEAD_DIM)

    query_blocks = block_view(queries)
    key_blocks = block_view(keys)
    value_blocks = block_view(values)
    causal = jnp.tril(jnp.ones((BLK, BLK), jnp.bool_))
    raw_scores = jnp.einsum("bthd,bshd->bhts", query_blocks, key_blocks, preferred_element_type=f32)
    scores = jnp.where(causal, raw_scores, 0.0).astype(jnp.bfloat16)
    block_states = jnp.einsum(
        "bthd,bthe->bhde", key_blocks, value_blocks, preferred_element_type=f32
    )
    own_total = jnp.sum(block_states, axis=0)
    empty_state = jnp.zeros_like(own_total)
    my_rank = lax.axis_index("seq")
    shards = lax.all_gather(own_total[None], "seq", axis=0, tiled=True)
    shard_rank = jnp.arange(shards.shape[0])
    keep_mask = (shard_rank < my_rank)[:, None, None, None]
    before = jnp.sum(jnp.where(keep_mask, shards, 0.0), axis=0)
    inside_before = jnp.concatenate(
        [empty_state[None], jnp.cumsum(block_states, axis=0)[:-1]], axis=0
    )
    prefixes = (before[None] + inside_before).astype(jnp.bfloat16)
    attended = jnp.einsum("bthd,bhde->bthe", query_blocks, prefixes, preferred_element_type=f32)
    attended = attended + jnp.einsum(
        "bhts,bshe->bthe", scores, value_blocks, preferred_element_type=f32
    )
    attended = attended.reshape(tok_rows, head_count * HEAD_DIM)
    grad_out = out_grad.astype(f32)
    scaled = gain[None, :] * grad_out
    square_sum, inner_sum = lax.psum(
        (jnp.sum(attended * attended, axis=1), jnp.sum(scaled * attended, axis=1)), "tp"
    )
    full_width = HEADS * HEAD_DIM
    inverse = lax.rsqrt(square_sum / full_width + epsilon)[:, None]
    attn_grad = (
        inverse * scaled
        - attended * inverse * inverse * inverse * (inner_sum / full_width)[:, None]
    ).astype(jnp.bfloat16)
    gain_grad = lax.psum(jnp.sum(grad_out * attended * inverse, axis=0), "seq")
    grad_blocks = block_view(attn_grad)
    grad_states = jnp.einsum(
        "bthd,bthe->bhde", query_blocks, grad_blocks, preferred_element_type=f32
    )
    own_grad = jnp.sum(grad_states, axis=0)
    after_sum = entering(own_grad, "seq", add_states, empty_state)
    inside_after = jnp.cumsum(grad_states[::-1], axis=0)[::-1]
    inside_after = jnp.concatenate([inside_after[1:], empty_state[None]], axis=0)
    suffixes = (after_sum[None] + inside_after).astype(jnp.bfloat16)
    mixing = jnp.where(
        causal,
        jnp.einsum("bthe,bshe->bhts", grad_blocks, value_blocks, preferred_element_type=f32),
        0.0,
    ).astype(jnp.bfloat16)
    query_grad = jnp.einsum("bthe,bhde->bthd", grad_blocks, prefixes, preferred_element_type=f32)
    query_grad = query_grad + jnp.einsum(
        "bhts,bshd->bthd", mixing, key_blocks, preferred_element_type=f32
    )
    key_grad = jnp.einsum("bthe,bhde->bthd", value_blocks, suffixes, preferred_element_type=f32)
    key_grad = key_grad + jnp.einsum(
        "bhts,bthd->bshd", mixing, query_blocks, preferred_element_type=f32
    )
    value_grad = jnp.einsum("bthd,bhde->bthe", key_blocks, suffixes, preferred_element_type=f32)
    value_grad = value_grad + jnp.einsum(
        "bhts,bthe->bshe", scores, grad_blocks, preferred_element_type=f32
    )
    shape_out = (tok_rows, head_count * HEAD_DIM)
    return (
        query_grad.reshape(shape_out).astype(jnp.bfloat16),
        key_grad.reshape(shape_out).astype(jnp.bfloat16),
        value_grad.reshape(shape_out).astype(jnp.bfloat16),
        gain_grad,
    )


def solution(mesh):
    in_specs = (P("seq", "tp"), P("seq", "tp"), P("seq", "tp"), P("seq", "tp"), P("tp"))
    out_specs = (P("seq", "tp"), P("seq", "tp"), P("seq", "tp"), P("tp"))
    return jax.shard_map(local, mesh=mesh, in_specs=in_specs, out_specs=out_specs, check_vma=False)
```

profile of v0, /device:TPU:1, one launch (start us, length us, event | category | flops | bytes accessed | tf_op | source)
XLA Modules:
  0.0 384.8 jit_solution(6092261023809970433)
XLA Ops:
  9.0 2.0 fusion.33
  11.5 1.5 fusion.35
  13.1 3.3 select_convert_fusion.1
  16.4 99.0 %all-gather.5.cloned.1.call-done = f32[256,128,128]{2,1,0:T(8,128)} async-done(((f32[4,128,128]{2,1,0:T(8,128)}), f32[256,128,128]{2,1,0:T(8,128)}) %all-gather.5.cloned.1.call-update) | async-done | bytes 16777232 | tf_op jit(solution)/shard_map/all_gather | solution.py:53
  115.4 8.4 %select_reduce_fusion = f32[4,128,128]{2,1,0:T(8,128)S(1)} fusion(f32[64,4,128,128]{3,2,1,0:T(8,128)} %bitcast.69, pred[64]{0:T(512)(128)(4,1)S(1)} %iota_compare_fusion.1), kind=kLoop, calls=%fused_computation.1 | loop fusion | flops 8323072 | bytes 17039424 | tf_op jit(solution)/shard_map/reduce_sum | solution.py:56
  123.8 1.8 fusion.23
  125.7 2.9 multiply_reduce_fusion
  128.6 8.4 %psum.21 = f32[1024]{0:T(1024)S(1)} all-reduce(f32[1024]{0:T(1024)S(1)} %bitcast.76), channel_id=1, replica_groups=mesh['seq'=64,'tp'=4] {'tp'}, use_global_device_ids=true, to_apply=%region_4.5 | all-reduce | flops 1024 | bytes 8192 | tf_op jit(solution)/shard_map/psum | solution.py:68
  137.0 2.1 copy.64
  140.0 6.0 %psum.22 = f32[1024]{0:T(1024)S(1)} all-reduce(f32[1024]{0:T(1024)S(1)} %get-tuple-element.131), channel_id=1, replica_groups=mesh['seq'=64,'tp'=4] {'tp'}, use_global_device_ids=true, to_apply=%region_6.7 | all-reduce | flops 1024 | bytes 8192 | tf_op jit(solution)/shard_map/psum | solution.py:68
  146.0 1.6 fusion.3
  151.9 1.5 fusion.30
  153.5 1.4 select_convert_fusion
  154.9 1.9 copy-done.1
  156.9 2.5 fusion.11
  159.3 2.4 copy.70
  161.7 2.4 copy.132
  164.1 128.9 %psum.23 = f32[512]{0:T(512)} all-reduce(f32[512]{0:T(512)S(1)} %get-tuple-element.130), channel_id=1, replica_groups=mesh['seq'=64,'tp'=4] {'seq'}, use_global_device_ids=true, to_apply=%region_12.13 | all-reduce | flops 512 | bytes 4096 | tf_op jit(solution)/shard_map/psum | solution.py:77
  293.1 4.3 %fusion.36 = f32[2,4,128,512]{3,2,1,0:T(8,128)} fusion(bf16[2,512,4,128]{1,3,2,0:T(8,128)(2,1)S(1)} %copy.71, bf16[2,4,512,512]{3,2,1,0:T(8,128)(2,1)} %select_convert_fusion.1), kind=kOutput, calls=%fused_computation.58 | convolution fusion | flops 536870912 | bytes 7340032 | tf_op jit(solution)/shard_map/bhts,bthe->bshe/dot_general | solution.py:101
  297.4 68.5 %while.16 = (s32[]{:T(128)}, f32[4,128,128]{2,1,0:T(8,128)S(1)}, s32[]{:T(128)}, f32[64,4,128,128]{3,2,1,0:T(8,128)}, s32[]{:T(128)}, /*index=5*/s32[]{:T(128)}, s32[]{:T(128)}, s32[]{:T(128)}) while((s32[]{:T(128)}, f32[4,128,128]{2,1,0:T(8,128)S(1)}, s32[]{:T(128)}, f32[64,4,128,128]{3,2,1,0:T(8,128)}, s32[]{:T(128)}, ...), condition=%wide.region_9.10_spmd.clone, body=%wide.region_8.9_spmd.clone.sunk | while | flops 196616 | bytes 786595 | solution.py:25
  366.2 1.8 fusion.26
  369.9 4.6 %fusion.10 = bf16[2,512,4,128]{1,3,2,0:T(8,128)(2,1)} fusion(f32[2,4,128,512]{3,2,1,0:T(8,128)} %fusion.26, bf16[2,4,512,512]{3,2,1,0:T(8,128)(2,1)} %copy-done.1, bf16[2,512,4,128]{3,2,1,0:T(4,128)(2,1)S(1)} %copy-done.3), kind=kOutput, calls=%fused_computation.18 | convolution fusion | flops 537919488 | bytes 8388608 | tf_op jit(solution)/shard_map/bhts,bthd->bshd/dot_general | solution.py:97
  374.6 1.7 copy.80
  376.3 1.7 copy_bitcast_fusion
  (130 shorter events, 76.2 us)
Async XLA Ops:
  7.2 1.5 copy-start.15
  7.2 108.2 %all-gather.5.cloned.1.call-start = ((), (), s32[]{:S(2)}) async-start(), calls=%async_computation | async-start | bytes 17039360 | tf_op jit(solution)/shard_map/all_gather | solution.py:53
  8.7 4.4 %copy-start.7 = (bf16[2,512,4,128]{3,2,1,0:T(4,128)(2,1)}, bf16[2,512,4,128]{3,2,1,0:T(4,128)(2,1)S(1)}, u32[]{:S(2)}) copy-start(bf16[2,512,4,128]{3,2,1,0:T(4,128)(2,1)S(1)} %reshape.39) | copy-start | bytes 3145732
  9.0 2.2 copy-start.4
  9.0 2.2 copy-start.16
  11.1 286.3 %all-gather.7.cloned.1.call-start = ((), (), s32[]{:S(2)}) async-start(), calls=%async_computation.1 | async-start | bytes 17039360 | tf_op jit(solution)/shard_map/all_gather | solution.py:16
  11.5 4.9 %copy-start.2 = (bf16[2,512,4,128]{3,2,1,0:T(4,128)(2,1)}, bf16[2,512,4,128]{3,2,1,0:T(4,128)(2,1)S(1)}, u32[]{:S(2)}) copy-start(bf16[2,512,4,128]{3,2,1,0:T(4,128)(2,1)S(1)} %reshape.41) | copy-start | bytes 3145732
  13.0 110.8 %copy-start.13 = (f32[1,4,128,128]{3,2,1,0:T(8,128)}, f32[1,4,128,128]{3,2,1,0:T(8,128)S(1)}, u32[]{:S(2)}) copy-start(f32[1,4,128,128]{3,2,1,0:T(8,128)S(1)} %slice.7) | copy-start | bytes 786436
  13.1 3.3 copy-start.17
  115.4 10.3 %copy-start = (bf16[2,4,512,512]{3,2,1,0:T(8,128)(2,1)S(1)}, bf16[2,4,512,512]{3,2,1,0:T(8,128)(2,1)}, u32[]{:S(2)}) copy-start(bf16[2,4,512,512]{3,2,1,0:T(8,128)(2,1)} %select_convert_fusion.1) | copy-start | bytes 12582916
  123.8 4.8 %copy-start.12 = (f32[4,128,128]{2,1,0:T(8,128)}, f32[4,128,128]{2,1,0:T(8,128)S(1)}, u32[]{:S(2)}) copy-start(f32[4,128,128]{2,1,0:T(8,128)S(1)} %select_reduce_fusion) | copy-start | bytes 786436
  123.8 1.9 copy-start.5
  137.0 2.1 copy-start.11
  137.0 2.1 copy-start.19
  147.6 2.1 copy-start.3
  151.9 1.6 copy-start.6
  151.9 1.6 copy-start.18
  153.5 3.4 copy-start.8
  154.9 1.9 copy-start.1
  297.4 68.6 %copy-start.14 = (f32[2,4,128,128]{2,3,1,0:T(8,128)S(1)}, f32[2,4,128,128]{2,3,1,0:T(8,128)}, u32[]{:S(2)}) copy-start(f32[2,4,128,128]{2,3,1,0:T(8,128)} %rev.4) | copy-start | bytes 1572868
  297.4 68.6 %copy-start.20 = (pred[2]{0:T(512)(128)(4,1)S(1)}, pred[2]{0:T(512)(128)(4,1)}, u32[]{:S(2)}) copy-start(pred[2]{0:T(512)(128)(4,1)} %constant.68.clone.1) | copy-start | bytes 10
  366.0 2.0 copy-start.9
  366.0 2.6 copy-start.10
Sparse Core Ops, SparseCore 0:
  11.2 104.1 all-gather.4
  151.2 99.9 all-gather.6
where the time goes:
time: 387 us; the launch traced here: 385 us
  blocking collectives  143 us (37%)
  waiting for transfers between devices  99 us (26%)
  other arithmetic  79.2 us (20%)
  matrix products  27.2 us (7%)
  local copies, waits for them, and re-layouts  19.7 us (5%)
  between operations  14.4 us (4%)
    psum x1, blocking collectives, local(): gain_grad = lax.psum(jnp.sum(grad_out * attended * inverse, axis=0), 'seq')  129 us
    all_gather x1, waiting for transfers between devices, local(): shards = lax.all_gather(own_total[None], 'seq', axis=0, tiled=True)  99 us
    select_n x64, other arithmetic, step(): return jnp.where(reached, new, before)  66.6 us
    psum x2, blocking collectives, local(): lax.psum((jnp.sum(attended * attended, axis=1), jnp.sum(scaled * attended...  14.4 us
    reduce_sum x1, other arithmetic, local(): before = jnp.sum(jnp.where(keep_mask, shards, 0.0), axis=0)  8.4 us
  transfers between devices with their start and end apart: 2, of which 1 were waited for; matrix products, arithmetic and copies ran while one was open for 5% of the time, Pallas kernels for 0%

commit v1 on v0

v1 whole, which is shorter than its diff:
```python
import jax
import jax.numpy as jnp
from jax import lax
from jax.experimental import pallas as pl
from jax.experimental.pallas import tpu as pltpu
from jax.sharding import PartitionSpec as P

HEAD_DIM = 128
BLK = 512
HALF = 256
NH = 4
TOK = 1024
FEAT = 512
FULL = 2048.0
YS = 4
ZS = 8
CHIPS = YS * ZS
PIECE = 8
EPS = 1e-05
MESH = pl.DeviceIdType.MESH
F32 = jnp.float32
BF16 = jnp.bfloat16

FIRST_SPLIT = 5
SECOND_SPLIT = 4


def ring(n, d):
    return min(d, n - d)


OFFSETS = sorted(
    [(dy, dz) for dy in range(YS) for dz in range(ZS) if (dy, dz) != (0, 0)],
    key=lambda o: -(ring(YS, o[0]) + ring(ZS, o[1])),
)


def dot_nn(a, b):
    return lax.dot_general(a, b, (((1,), (0,)), ((), ())), preferred_element_type=F32)


def dot_nt(a, b):
    return lax.dot_general(a, b, (((1,), (1,)), ((), ())), preferred_element_type=F32)


def dot_tn(a, b):
    return lax.dot_general(a, b, (((0,), (0,)), ((), ())), preferred_element_type=F32)


def kernel(
    q_hbm, k_hbm, v_hbm, g_hbm, gain_ref,
    qg_ref, kg_ref, vg_ref, gg_ref,
    q, k, v, g, sc, att, da, kga, vga,
    inside, total, sib, piece, rb1, ob1, rb2, xb, edge, pref,
    tpo, tpr, gacc, gown, gsib, gchip, gz, gzs, gy,
    load_sem, send_sem, recv_sem,
):
    me = lax.axis_index("seq")
    tp = lax.axis_index("tp")
    chip = me // 2
    core = me % 2
    yy = chip // ZS
    zz = chip % ZS
    sibling = (me + 1 - 2 * core, tp)

    def chip_at(dy, dz):
        return (yy + dy) % YS * ZS + (zz + dz) % ZS

    chips = [chip_at(dy, dz) for dy, dz in OFFSETS]
    tps = [(me, (tp + d) % 4) for d in (2, 1, 3)]

    barrier = pltpu.get_barrier_semaphore()
    for c in chips:
        pl.semaphore_signal(barrier, inc=1, device_id=(2 * c + core, tp), device_id_type=MESH)
    for t in tps:
        pl.semaphore_signal(barrier, inc=1, device_id=t, device_id_type=MESH)
    pl.semaphore_signal(barrier, inc=1, device_id=sibling, device_id_type=MESH)

    loads = [
        pltpu.make_async_copy(src, dst, load_sem.at[i])
        for i, (src, dst) in enumerate(((k_hbm, k), (v_hbm, v), (q_hbm, q), (g_hbm, g)))
    ]
    for load in loads:
        load.start()

    def remote(src, dst, index, device):
        return pltpu.make_async_remote_copy(
            src_ref=src, dst_ref=dst, send_sem=send_sem.at[index], recv_sem=recv_sem.at[index],
            device_id=device, device_id_type=MESH,
        )

    def rows(i, n):
        return pl.ds(pl.multiple_of(i * n, n), n)

    row_id = lax.broadcasted_iota(jnp.int32, (HALF, HALF), 0)
    col_id = lax.broadcasted_iota(jnp.int32, (HALF, HALF), 1)
    causal = col_id <= row_id

    def where_at(u):
        b = u // NH
        h = u % NH
        start = pl.multiple_of(b * BLK, BLK)
        return b, h, start, pl.ds(pl.multiple_of(h * HEAD_DIM, HEAD_DIM), HEAD_DIM)

    def states(left, right, scan, inner):
        def body(h, carry):
            cols = pl.ds(pl.multiple_of(h * HEAD_DIM, HEAD_DIM), HEAD_DIM)
            first = dot_tn(left[pl.ds(0, BLK), cols], right[pl.ds(0, BLK), cols])
            second = dot_tn(left[pl.ds(BLK, BLK), cols], right[pl.ds(BLK, BLK), cols])
            inside[scan, rows(h, HEAD_DIM), :] = second if inner == 1 else first
            total[scan, rows(h, HEAD_DIM), :] = first + second
            return carry

        lax.fori_loop(0, NH, body, 0, unroll=True)

    def score_unit(u, carry):
        b, h, start, cols = where_at(u)
        upper, lower, both = pl.ds(start, HALF), pl.ds(start + HALF, HALF), pl.ds(start, BLK)
        top = jnp.where(causal, dot_nt(q[upper, cols], k[upper, cols]), 0.0).astype(BF16)
        low = dot_nt(q[lower, cols], k[upper, cols]).astype(BF16)
        end = jnp.where(causal, dot_nt(q[lower, cols], k[lower, cols]), 0.0).astype(BF16)
        sc[u, pl.ds(0, HALF), pl.ds(0, HALF)] = top
        sc[u, pl.ds(HALF, HALF), pl.ds(0, HALF)] = low
        sc[u, pl.ds(HALF, HALF), pl.ds(HALF, HALF)] = end
        att[upper, cols] = dot_nn(top, v[upper, cols])
        att[lower, cols] = dot_nn(low, v[upper, cols]) + dot_nn(end, v[lower, cols])
        return carry

    def mixing_unit(u, carry):
        b, h, start, cols = where_at(u)
        upper, lower, both = pl.ds(start, HALF), pl.ds(start + HALF, HALF), pl.ds(start, BLK)
        d_up, d_low = da[upper, cols], da[lower, cols]
        top = jnp.where(causal, dot_nt(d_up, v[upper, cols]), 0.0).astype(BF16)
        low = dot_nt(d_low, v[upper, cols]).astype(BF16)
        end = jnp.where(causal, dot_nt(d_low, v[lower, cols]), 0.0).astype(BF16)
        before = pref[b, rows(h, HEAD_DIM), :]
        k_up, k_low = k[upper, cols], k[lower, cols]
        qg_ref[upper, cols] = (dot_nt(d_up, before) + dot_nn(top, k_up)).astype(BF16)
        qg_ref[lower, cols] = (
            dot_nt(d_low, before) + dot_nn(low, k_up) + dot_nn(end, k_low)
        ).astype(BF16)
        q_up, q_low = q[upper, cols], q[lower, cols]
        kga[upper, cols] = dot_tn(top, q_up) + dot_tn(low, q_low)
        kga[lower, cols] = dot_tn(end, q_low)
        s_top = sc[u, pl.ds(0, HALF), pl.ds(0, HALF)]
        s_low = sc[u, pl.ds(HALF, HALF), pl.ds(0, HALF)]
        s_end = sc[u, pl.ds(HALF, HALF), pl.ds(HALF, HALF)]
        vga[upper, cols] = dot_tn(s_top, d_up) + dot_tn(s_low, d_low)
        vga[lower, cols] = dot_tn(s_end, d_low)
        return carry

    mine = rows(core, HALF)
    other = rows(1 - core, HALF)

    def scan_sums(scan, base, work, split, forward, with_gain):
        copies = []
        give = remote(total.at[scan, other], sib.at[scan], base, sibling)
        give.start()
        if with_gain:
            give_gain = remote(gown, gsib, base + 4, sibling)
            give_gain.start()
        give.wait_recv()
        piece[scan] = total[scan, mine, :] + sib[scan]
        for c in chips:
            remote(
                piece.at[scan, rows(c, PIECE)], rb1.at[scan, rows(chip, PIECE)], base + 1, (2 * c + core, tp)
            ).start()
        rb1[scan, rows(chip, PIECE), :] = piece[scan, rows(chip, PIECE), :]
        if with_gain:
            give_gain.wait_recv()
            gchip[...] = gown[...] + gsib[...]
            for d in (4, 3, 5, 2, 6, 1, 7):
                c = chip_at(0, d)
                remote(gchip, gz.at[zz], base + 5, (2 * c + core, tp)).start()
            gz[zz] = gchip[...]
        lax.fori_loop(0, split, work, 0)
        nothing = (CHIPS - 1) * PIECE
        wait1 = remote(piece.at[scan, pl.ds(0, nothing)], rb1.at[scan, pl.ds(0, nothing)], base + 1, sibling)
        wait1.wait_recv()
        running = jnp.zeros((PIECE, HEAD_DIM), F32)
        for i in range(CHIPS):
            at = pl.ds((i if forward else CHIPS - 1 - i) * PIECE, PIECE)
            ob1[scan, at, :] = running
            running = running + rb1[scan, at, :]
        for c in chips:
            remote(
                ob1.at[scan, rows(c, PIECE)], rb2.at[scan, rows(chip, PIECE)], base + 2, (2 * c + core, tp)
            ).start()
        rb2[scan, rows(chip, PIECE), :] = ob1[scan, rows(chip, PIECE), :]
        if with_gain:
            wait_z = remote(gz.at[pl.ds(0, ZS - 1)], gz.at[pl.ds(0, ZS - 1)], base + 5, sibling)
            wait_z.wait_recv()
            gzs[...] = jnp.sum(gz[...], axis=0)
            for d in (2, 1, 3):
                c = chip_at(d, 0)
                remote(gzs, gy.at[yy], base + 6, (2 * c + core, tp)).start()
            gy[yy] = gzs[...]
        lax.fori_loop(split, 2 * NH, work, 0)
        wait2 = remote(ob1.at[scan, pl.ds(0, nothing)], rb2.at[scan, pl.ds(0, nothing)], base + 2, sibling)
        wait2.wait_recv()
        late = core == 1 if forward else core == 0
        arrived = rb2[scan]
        xb[scan] = arrived + jnp.where(late, 0.0, total[scan, mine, :])
        swap = remote(xb.at[scan], edge.at[scan, mine], base + 3, sibling)
        swap.start()
        edge[scan, mine, :] = arrived + jnp.where(late, sib[scan], 0.0)
        swap.wait_recv()
        give.wait_send()
        wait1.wait_send()
        wait2.wait_send()
        swap.wait_send()
        if with_gain:
            give_gain.wait_send()
            wait_z.wait_send()
            wait_y = remote(gy.at[pl.ds(0, YS - 1)], gy.at[pl.ds(0, YS - 1)], base + 6, sibling)
            wait_y.wait_recv()
            wait_y.wait_send()
            gg_ref[...] = jnp.sum(gy[...], axis=0)[:NH]

    loads[0].wait()
    loads[1].wait()
    states(k, v, 0, 0)
    pl.semaphore_wait(barrier, CHIPS - 1 + 3 + 1)
    loads[2].wait()
    scan_sums(0, 0, score_unit, FIRST_SPLIT, True, False)
    loads[3].wait()

    pref[0] = edge[0].astype(BF16)
    pref[1] = (edge[0] + inside[0]).astype(BF16)
    eye = (
        lax.broadcasted_iota(jnp.int32, (HEAD_DIM, HEAD_DIM), 0)
        == lax.broadcasted_iota(jnp.int32, (HEAD_DIM, HEAD_DIM), 1)
    )

    def attend(i, carry):
        b = i // (BLK // HEAD_DIM)
        here = rows(i, HEAD_DIM)
        squares = jnp.zeros((HEAD_DIM, HEAD_DIM), F32)
        inner = jnp.zeros((HEAD_DIM, HEAD_DIM), F32)
        for h in range(NH):
            cols = pl.ds(h * HEAD_DIM, HEAD_DIM)
            a = att[here, cols] + dot_nn(q[here, cols], pref[b, pl.ds(h * HEAD_DIM, HEAD_DIM), :])
            att[here, cols] = a
            squares = squares + a * a
            inner = inner + gain_ref[:, cols] * g[here, cols].astype(F32) * a
        sq = jnp.sum(squares, axis=1, keepdims=True)
        inn = jnp.sum(inner, axis=1, keepdims=True)
        tpo[pl.ds(i, 1), :] = jnp.sum(jnp.where(eye, sq, 0.0), axis=0, keepdims=True)
        tpo[pl.ds(i + 8, 1), :] = jnp.sum(jnp.where(eye, inn, 0.0), axis=0, keepdims=True)
        return carry

    lax.fori_loop(0, TOK // HEAD_DIM, attend, 0, unroll=2)
    sends = [remote(tpo, tpr.at[i], 11 + i, t) for i, t in enumerate(tps)]
    for s in sends:
        s.start()
    for s in sends:
        s.wait_recv()
    sums = tpo[...] + tpr[0] + tpr[1] + tpr[2]
    for s in sends:
        s.wait_send()
    inverse = lax.rsqrt(sums[:8] / FULL + EPS)
    tpo[pl.ds(0, 8), :] = inverse
    tpo[pl.ds(8, 8), :] = inverse * inverse * inverse * (sums[8:] / FULL)
    gacc[...] = jnp.zeros_like(gacc)

    def grads(i, carry):
        here = rows(i, HEAD_DIM)
        r = jnp.sum(jnp.where(eye, tpo[pl.ds(i, 1), :], 0.0), axis=1, keepdims=True)
        m = jnp.sum(jnp.where(eye, tpo[pl.ds(i + 8, 1), :], 0.0), axis=1, keepdims=True)
        for h in range(NH):
            cols = pl.ds(h * HEAD_DIM, HEAD_DIM)
            a = att[here, cols]
            gr = g[here, cols].astype(F32) * r
            da[here, cols] = (gain_ref[:, cols] * gr - a * m).astype(BF16)
            gacc[h] += jnp.sum((gr * a).reshape(HEAD_DIM // 8, 8, HEAD_DIM), axis=0)
        return carry

    lax.fori_loop(0, TOK // HEAD_DIM, grads, 0, unroll=2)
    states(q, da, 1, 1)
    for h in range(NH):
        gown[pl.ds(h, 1), :] = jnp.sum(gacc[h], axis=0, keepdims=True)
        gown[pl.ds(h + NH, 1), :] = jnp.zeros((1, HEAD_DIM), F32)
    scan_sums(1, 4, mixing_unit, SECOND_SPLIT, False, True)

    pref[0] = (edge[1] + inside[1]).astype(BF16)
    pref[1] = edge[1].astype(BF16)

    def finish(u, carry):
        b, h, start, cols = where_at(u)
        both = pl.ds(start, BLK)
        after = pref[b, rows(h, HEAD_DIM), :]
        kg_ref[both, cols] = (dot_nt(v[both, cols], after) + kga[both, cols]).astype(BF16)
        vg_ref[both, cols] = (dot_nn(k[both, cols], after) + vga[both, cols]).astype(BF16)
        return carry

    lax.fori_loop(0, 2 * NH, finish, 0, unroll=2)


def local(queries, keys, values, out_grad, gain):
    vmem = pltpu.VMEM
    big = jax.ShapeDtypeStruct((TOK, FEAT), BF16)
    state = (2, NH * HEAD_DIM, HEAD_DIM)
    half = (2, HALF, HEAD_DIM)
    tile = (8, HEAD_DIM)
    anywhere = pl.BlockSpec(memory_space=pl.ANY)
    whole = pl.BlockSpec(memory_space=vmem)
    out = pl.pallas_call(
        kernel,
        name="attention_backward",
        out_shape=(big, big, big, jax.ShapeDtypeStruct((NH, HEAD_DIM), F32)),
        in_specs=[anywhere] * 4 + [whole],
        out_specs=(whole,) * 4,
        scratch_shapes=[
            vmem((TOK, FEAT), BF16),
            vmem((TOK, FEAT), BF16),
            vmem((TOK, FEAT), BF16),
            vmem((TOK, FEAT), BF16),
            vmem((2 * NH, BLK, BLK), BF16),
            vmem((TOK, FEAT), F32),
            vmem((TOK, FEAT), BF16),
            vmem((TOK, FEAT), F32),
            vmem((TOK, FEAT), F32),
            vmem(state, F32),
            vmem(state, F32),
            vmem(half, F32),
            vmem(half, F32),
            vmem(half, F32),
            vmem(half, F32),
            vmem(half, F32),
            vmem(half, F32),
            vmem(state, F32),
            vmem(state, BF16),
            vmem((16, HEAD_DIM), F32),
            vmem((3, 16, HEAD_DIM), F32),
            vmem((NH, 8, HEAD_DIM), F32),
            vmem(tile, F32),
            vmem(tile, F32),
            vmem(tile, F32),
            vmem((ZS, 8, HEAD_DIM), F32),
            vmem(tile, F32),
            vmem((YS, 8, HEAD_DIM), F32),
            pltpu.SemaphoreType.DMA((4,)),
            pltpu.SemaphoreType.DMA((14,)),
            pltpu.SemaphoreType.DMA((14,)),
        ],
        compiler_params=pltpu.CompilerParams(
            collective_id=0, has_side_effects=True, vmem_limit_bytes=48 * 1024 * 1024
        ),
    )(queries, keys, values, out_grad, gain.reshape(1, FEAT))
    return out[0], out[1], out[2], out[3].reshape(FEAT)


def solution(mesh):
    in_specs = (P("seq", "tp"), P("seq", "tp"), P("seq", "tp"), P("seq", "tp"), P("tp"))
    out_specs = (P("seq", "tp"), P("seq", "tp"), P("seq", "tp"), P("tp"))
    return jax.shard_map(local, mesh=mesh, in_specs=in_specs, out_specs=out_specs, check_vma=False)
```

time: 387 us -> 56 us (0.14)
  blocking collectives: 143 us -> 0 us
  waiting for transfers between devices: 99 us -> 0 us
  other arithmetic: 79.2 us -> 0 us
  Pallas kernels: 0 us -> 48.5 us
  matrix products: 27.2 us -> 0 us
  between operations: 14.4 us -> 0.65 us
  local copies, waits for them, and re-layouts: 19.7 us -> 6.61 us
    psum x3 -> x0, blocking collectives: 143 us -> none  [the longest x1 129 us: local(): gain_grad = lax.psum(jnp.sum(grad_out * attended * inverse, axis=0), 'seq')]
    all_gather x2 -> x0, waiting for transfers between devices: 99 us -> none  [the longest x1 99 us: local(): shards = lax.all_gather(own_total[None], 'seq', axis=0, tiled=True)]
    select_n x64 -> x0, other arithmetic: 66.6 us -> none  [step(): return jnp.where(reached, new, before)]
    pallas_call x0 -> x1, Pallas kernels: none -> 48.5 us  [local(): pl.pallas_call(kernel, name='attention_backward', out_shape=(big, big, bi...]
    dot_general x12 -> x0, matrix products: 27.2 us -> none  [the longest x1 4.65 us: local(): jnp.einsum('bhts,bthd->bshd', mixing, query_blocks, preferred_element_typ...]
    reduce_sum x2 -> x0, other arithmetic: 9.28 us -> none  [the longest x1 8.4 us: local(): before = jnp.sum(jnp.where(keep_mask, shards, 0.0), axis=0)]
    convert_element_type x4 -> x0, local copies, waits for them, and re-layouts: 6.5 us -> none  [the longest x2 2.42 us: local(): value_grad.reshape(shape_out).astype(jnp.bfloat16)]
    reshape x5 -> x0, local copies, waits for them, and re-layouts: 4.08 us -> none  [block_view(): return array.reshape(block_count, BLK, head_count, HEAD_DIM)]
  transfers between devices with their start and end apart: 2 -> 0, of which waited for: 1 -> 0; matrix products, arithmetic and copies ran while one was open for 5% -> 0% of each run, Pallas kernels for 0% -> 0%
where the time goes in v1:
time: 56 us; the launch traced here: 55.8 us
  Pallas kernels  48.5 us (87%)
  local copies, waits for them, and re-layouts  6.61 us (12%)
  between operations  0.65 us (1%)
    pallas_call x1, Pallas kernels, local(): pl.pallas_call(kernel, name='attention_backward', out_shape=(big, big, bi...  48.5 us
    unnamed x10, local copies, waits for them, and re-layouts  6.61 us

profile of v1, /device:TPU:1, one launch (start us, length us, event | category | flops | bytes accessed | tf_op | source)
XLA Modules:
  0.0 55.8 jit_solution(9628361896407141824)
XLA Ops:
  0.6 0.0 copy-start
  0.6 1.2 %copy-done = bf16[1024,512]{1,0:T(8,128)(2,1)S(1)} copy-done((bf16[1024,512]{1,0:T(8,128)(2,1)S(1)}, bf16[1024,512]{1,0:T(8,128)(2,1)}, u32[]{:S(2)}) %copy-start) | copy-done | bytes 1048600
  1.9 0.0 copy-start.1
  1.9 1.2 %copy-done.1 = bf16[1024,512]{1,0:T(8,128)(2,1)S(1)} copy-done((bf16[1024,512]{1,0:T(8,128)(2,1)S(1)}, bf16[1024,512]{1,0:T(8,128)(2,1)}, u32[]{:S(2)}) %copy-start.1) | copy-done | bytes 1048600
  3.1 0.0 copy-start.2
  3.1 0.7 %copy-done.2 = f32[512]{0:T(512)S(1)} copy-done((f32[512]{0:T(512)S(1)}, f32[512]{0:T(512)}, u32[]{:S(2)}) %copy-start.2) | copy-done | bytes 2072
  3.8 48.5 %attention_backward.1 = (bf16[1024,512]{1,0:T(8,128)(2,1)S(1)}, bf16[1024,512]{1,0:T(8,128)(2,1)S(1)}, bf16[1024,512]{1,0:T(8,128)(2,1)S(1)}, f32[4,128]{1,0:T(4,128)S(1)}) custom-call(bf16[1024,512]{1,0:T(8,128)(2,1)S(1)} %copy-done, bf16[1024,512]{1,0:T(8,128)(2,1)S(1)} %copy-done.1, bf16[1024,512]{1,0:T(8,128)(2,1)} %v_hbm.1, bf16[1024,512]{1,0:T(8,128)(2,1)} %g_hbm.1, ...), custom_call_target="tpu_custom_call" | custom-call | tf_op jit(solution)/shard_map/attention_backward/pallas_call | solution.py:307
  52.3 1.0 %copy.13 = bf16[1024,512]{1,0:T(8,128)(2,1)} copy(bf16[1024,512]{1,0:T(8,128)(2,1)S(1)} %get-tuple-element.16) | data formatting | bytes 2097152
  53.3 1.0 %copy.14 = bf16[1024,512]{1,0:T(8,128)(2,1)} copy(bf16[1024,512]{1,0:T(8,128)(2,1)S(1)} %get-tuple-element.17) | data formatting | bytes 2097152
  54.2 1.0 %copy.15 = bf16[1024,512]{1,0:T(8,128)(2,1)} copy(bf16[1024,512]{1,0:T(8,128)(2,1)S(1)} %get-tuple-element.18) | data formatting | bytes 2097152
  55.2 0.6 %copy.16 = f32[512]{0:T(512)} copy(f32[512]{0:T(512)S(1)} %bitcast.3) | data formatting | bytes 4096
Async XLA Ops:
  0.6 1.2 %copy-start = (bf16[1024,512]{1,0:T(8,128)(2,1)S(1)}, bf16[1024,512]{1,0:T(8,128)(2,1)}, u32[]{:S(2)}) copy-start(bf16[1024,512]{1,0:T(8,128)(2,1)} %q_hbm.1) | copy-start | bytes 3145732
  1.9 1.2 %copy-start.1 = (bf16[1024,512]{1,0:T(8,128)(2,1)S(1)}, bf16[1024,512]{1,0:T(8,128)(2,1)}, u32[]{:S(2)}) copy-start(bf16[1024,512]{1,0:T(8,128)(2,1)} %k_hbm.1) | copy-start | bytes 3145732
  3.1 0.7 %copy-start.2 = (f32[512]{0:T(512)S(1)}, f32[512]{0:T(512)}, u32[]{:S(2)}) copy-start(f32[512]{0:T(512)} %param.9) | copy-start | bytes 6148

commit v2 on v1

v2 whole, which is shorter than its diff:
```python
import jax
import jax.numpy as jnp
from jax import lax
from jax.experimental import pallas as pl
from jax.experimental.pallas import tpu as pltpu
from jax.sharding import PartitionSpec as P

HEAD_DIM = 128
BLK = 512
HALF = 256
NH = 4
TOK = 1024
FEAT = 512
FULL = 2048.0
YS = 4
ZS = 8
CHIPS = YS * ZS
PIECE = 8
EPS = 1e-05
MESH = pl.DeviceIdType.MESH
F32 = jnp.float32
BF16 = jnp.bfloat16

FIRST_SPLIT = 5
SECOND_SPLIT = 4
UNROLL = 8


def ring(n, d):
    return min(d, n - d)


OFFSETS = sorted(
    [(dy, dz) for dy in range(YS) for dz in range(ZS) if (dy, dz) != (0, 0)],
    key=lambda o: -(ring(YS, o[0]) + ring(ZS, o[1])),
)


def dot_nn(a, b):
    return lax.dot_general(a, b, (((1,), (0,)), ((), ())), preferred_element_type=F32)


def dot_nt(a, b):
    return lax.dot_general(a, b, (((1,), (1,)), ((), ())), preferred_element_type=F32)


def dot_tn(a, b):
    return lax.dot_general(a, b, (((0,), (0,)), ((), ())), preferred_element_type=F32)


def kernel(
    q_hbm, k_hbm, v_hbm, g_hbm, gain_hbm,
    qg_ref, kg_ref, vg_ref, gg_ref,
    q, k, v, g, gain, sc, att, scaled, da, kga, vga, rcol, mcol,
    inside, total, sib, piece, rb1, ob1, rb2, xb, edge, pref,
    tpo, tpr, gchip, gz, gzs, gy,
    load_sem, send_sem, recv_sem,
):
    me = lax.axis_index("seq")
    tp = lax.axis_index("tp")
    chip = me // 2
    core = me % 2
    yy = chip // ZS
    zz = chip % ZS
    sibling = (me + 1 - 2 * core, tp)

    def chip_at(dy, dz):
        return (yy + dy) % YS * ZS + (zz + dz) % ZS

    chips = [chip_at(dy, dz) for dy, dz in OFFSETS]
    crossed = [(2 * chip_at(dy, 0) + 1 - core, tp) for dy in (2, 1, 3)]
    tps = [(me, (tp + d) % 4) for d in (2, 1, 3)]

    barrier = pltpu.get_barrier_semaphore()
    peers = [(2 * c + core, tp) for c in chips] + crossed + tps + [sibling]
    for p in peers:
        pl.semaphore_signal(barrier, inc=1, device_id=p, device_id_type=MESH)

    loads = [
        pltpu.make_async_copy(src, dst, load_sem.at[i])
        for i, (src, dst) in enumerate(
            ((k_hbm, k), (v_hbm, v), (q_hbm, q), (g_hbm, g), (gain_hbm, gain))
        )
    ]
    for load in loads:
        load.start()

    def remote(src, dst, index, device):
        return pltpu.make_async_remote_copy(
            src_ref=src, dst_ref=dst, send_sem=send_sem.at[index], recv_sem=recv_sem.at[index],
            device_id=device, device_id_type=MESH,
        )

    def rows(i, n):
        return pl.ds(pl.multiple_of(i * n, n), n)

    row_id = lax.broadcasted_iota(jnp.int32, (HALF, HALF), 0)
    col_id = lax.broadcasted_iota(jnp.int32, (HALF, HALF), 1)
    causal = col_id <= row_id
    eye = (
        lax.broadcasted_iota(jnp.int32, (HEAD_DIM, HEAD_DIM), 0)
        == lax.broadcasted_iota(jnp.int32, (HEAD_DIM, HEAD_DIM), 1)
    )
    mine = rows(core, HALF)
    other = rows(1 - core, HALF)
    own_heads = [2 * core, 2 * core + 1]
    other_heads = [2 - 2 * core, 3 - 2 * core]

    def where_at(u):
        b = u // NH
        h = u % NH
        start = pl.multiple_of(b * BLK, BLK)
        return b, h, start, rows(h, HEAD_DIM)

    def states(heads, left, right, scan, inner):
        for h in heads:
            cols = rows(h, HEAD_DIM)
            first = dot_tn(left[pl.ds(0, BLK), cols], right[pl.ds(0, BLK), cols])
            second = dot_tn(left[pl.ds(BLK, BLK), cols], right[pl.ds(BLK, BLK), cols])
            inside[scan, cols, :] = second if inner == 1 else first
            total[scan, cols, :] = first + second

    def score_unit(u, carry):
        b, h, start, cols = where_at(u)
        upper, lower, both = pl.ds(start, HALF), pl.ds(start + HALF, HALF), pl.ds(start, BLK)
        top = jnp.where(causal, dot_nt(q[upper, cols], k[upper, cols]), 0.0).astype(BF16)
        low = dot_nt(q[lower, cols], k[upper, cols]).astype(BF16)
        end = jnp.where(causal, dot_nt(q[lower, cols], k[lower, cols]), 0.0).astype(BF16)
        sc[u, pl.ds(0, HALF), pl.ds(0, HALF)] = top
        sc[u, pl.ds(HALF, HALF), pl.ds(0, HALF)] = low
        sc[u, pl.ds(HALF, HALF), pl.ds(HALF, HALF)] = end
        att[upper, cols] = dot_nn(top, v[upper, cols])
        att[lower, cols] = dot_nn(low, v[upper, cols]) + dot_nn(end, v[lower, cols])
        scaled[both, cols] = gain[:, cols] * g[both, cols].astype(F32)
        return carry

    def mixing_unit(u, carry):
        b, h, start, cols = where_at(u)
        upper, lower, both = pl.ds(start, HALF), pl.ds(start + HALF, HALF), pl.ds(start, BLK)
        d_up, d_low = da[upper, cols], da[lower, cols]
        top = jnp.where(causal, dot_nt(d_up, v[upper, cols]), 0.0).astype(BF16)
        low = dot_nt(d_low, v[upper, cols]).astype(BF16)
        end = jnp.where(causal, dot_nt(d_low, v[lower, cols]), 0.0).astype(BF16)
        before = pref[0, b, cols, :]
        k_up, k_low = k[upper, cols], k[lower, cols]
        qg_ref[upper, cols] = (dot_nt(d_up, before) + dot_nn(top, k_up)).astype(BF16)
        qg_ref[lower, cols] = (
            dot_nt(d_low, before) + dot_nn(low, k_up) + dot_nn(end, k_low)
        ).astype(BF16)
        q_up, q_low = q[upper, cols], q[lower, cols]
        kga[upper, cols] = dot_tn(top, q_up) + dot_tn(low, q_low)
        kga[lower, cols] = dot_tn(end, q_low)
        s_top = sc[u, pl.ds(0, HALF), pl.ds(0, HALF)]
        s_low = sc[u, pl.ds(HALF, HALF), pl.ds(0, HALF)]
        s_end = sc[u, pl.ds(HALF, HALF), pl.ds(HALF, HALF)]
        vga[upper, cols] = dot_tn(s_top, d_up) + dot_tn(s_low, d_low)
        vga[lower, cols] = dot_tn(s_end, d_low)
        return carry

    nothing = (CHIPS - 1) * PIECE

    def give_half(scan, base):
        give = remote(total.at[scan, other], sib.at[scan], base, sibling)
        give.start()
        return give

    def spread(scan, base, give):
        give.wait_recv()
        piece[scan] = total[scan, mine, :] + sib[scan]
        for c in chips:
            remote(
                piece.at[scan, rows(c, PIECE)], rb1.at[scan, rows(chip, PIECE)], base + 1, (2 * c + core, tp)
            ).start()
        rb1[scan, rows(chip, PIECE), :] = piece[scan, rows(chip, PIECE), :]
        return remote(piece.at[scan, pl.ds(0, nothing)], rb1.at[scan, pl.ds(0, nothing)], base + 1, sibling)

    def scan_back(scan, base, forward, wait1):
        wait1.wait_recv()
        running = jnp.zeros((PIECE, HEAD_DIM), F32)
        for i in range(CHIPS):
            at = pl.ds((i if forward else CHIPS - 1 - i) * PIECE, PIECE)
            ob1[scan, at, :] = running
            running = running + rb1[scan, at, :]
        for c in chips:
            remote(
                ob1.at[scan, rows(c, PIECE)], rb2.at[scan, rows(chip, PIECE)], base + 2, (2 * c + core, tp)
            ).start()
        rb2[scan, rows(chip, PIECE), :] = ob1[scan, rows(chip, PIECE), :]
        return remote(ob1.at[scan, pl.ds(0, nothing)], rb2.at[scan, pl.ds(0, nothing)], base + 2, sibling)

    def round_half(scan, half, forward):
        reach = edge[scan, half, :]
        further = (reach + inside[scan, half, :]).astype(BF16)
        pref[scan, 0 if forward else 1, half, :] = reach.astype(BF16)
        pref[scan, 1 if forward else 0, half, :] = further

    def swap_half(scan, base, forward, wait2):
        wait2.wait_recv()
        late = core == 1 if forward else core == 0
        arrived = rb2[scan]
        xb[scan] = arrived + jnp.where(late, 0.0, total[scan, mine, :])
        swap = remote(xb.at[scan], edge.at[scan, mine], base + 3, sibling)
        swap.start()
        edge[scan, mine, :] = arrived + jnp.where(late, sib[scan], 0.0)
        round_half(scan, mine, forward)
        return swap

    loads[0].wait()
    loads[1].wait()
    states(other_heads + own_heads, k, v, 0, 0)
    pl.semaphore_wait(barrier, len(peers))
    give = give_half(0, 0)
    loads[2].wait()
    loads[3].wait()
    loads[4].wait()
    wait1 = spread(0, 0, give)
    lax.fori_loop(0, FIRST_SPLIT, score_unit, 0)
    wait2 = scan_back(0, 0, True, wait1)
    lax.fori_loop(FIRST_SPLIT, 2 * NH, score_unit, 0)
    swap = swap_half(0, 0, True, wait2)

    def attend(heads, second):
        def body(i, carry):
            b = i // (BLK // HEAD_DIM)
            here = rows(i, HEAD_DIM)
            squares, inner = (rcol[here], mcol[here]) if second else (0.0, 0.0)
            for h in heads:
                cols = rows(h, HEAD_DIM)
                a = att[here, cols] + dot_nn(q[here, cols], pref[0, b, cols, :])
                att[here, cols] = a
                squares = squares + a * a
                inner = inner + scaled[here, cols] * a
            if second:
                sq = jnp.sum(squares, axis=1, keepdims=True)
                inn = jnp.sum(inner, axis=1, keepdims=True)
                tpo[pl.ds(i, 1), :] = jnp.sum(jnp.where(eye, sq, 0.0), axis=0, keepdims=True)
                tpo[pl.ds(i + 8, 1), :] = jnp.sum(jnp.where(eye, inn, 0.0), axis=0, keepdims=True)
            else:
                rcol[here] = squares
                mcol[here] = inner
            return carry

        lax.fori_loop(0, TOK // HEAD_DIM, body, 0, unroll=UNROLL)

    attend(own_heads, False)
    swap.wait_recv()
    round_half(0, other, True)
    attend(other_heads, True)
    sends = [remote(tpo, tpr.at[i], 11 + i, t) for i, t in enumerate(tps)]
    for s in sends:
        s.start()
    give.wait_send()
    wait1.wait_send()
    wait2.wait_send()
    swap.wait_send()
    for s in sends:
        s.wait_recv()
    sums = tpo[...] + tpr[0] + tpr[1] + tpr[2]
    for s in sends:
        s.wait_send()
    inverse = lax.rsqrt(sums[:8] / FULL + EPS)
    tpo[pl.ds(0, 8), :] = inverse
    tpo[pl.ds(8, 8), :] = inverse * inverse * inverse * (sums[8:] / FULL)

    def grads(heads, second):
        def body(i, carry):
            here = rows(i, HEAD_DIM)
            if second:
                r, m = rcol[here], mcol[here]
            else:
                r = jnp.sum(jnp.where(eye, tpo[pl.ds(i, 1), :], 0.0), axis=1, keepdims=True)
                m = jnp.sum(jnp.where(eye, tpo[pl.ds(i + 8, 1), :], 0.0), axis=1, keepdims=True)
                r = jnp.broadcast_to(r, (HEAD_DIM, HEAD_DIM))
                m = jnp.broadcast_to(m, (HEAD_DIM, HEAD_DIM))
                rcol[here] = r
                mcol[here] = m
            for h in heads:
                cols = rows(h, HEAD_DIM)
                da[here, cols] = (r * scaled[here, cols] - m * att[here, cols]).astype(BF16)
            return carry

        lax.fori_loop(0, TOK // HEAD_DIM, body, 0, unroll=UNROLL)

    grads(other_heads, False)
    states(other_heads, q, da, 1, 1)
    give = give_half(1, 4)
    grads(own_heads, True)
    states(own_heads, q, da, 1, 1)
    wait1 = spread(1, 4, give)

    def gains(i, carry):
        here = rows(i, HEAD_DIM)
        r = rcol[here]
        sums = []
        for h in range(NH):
            cols = pl.ds(h * HEAD_DIM, HEAD_DIM)
            term = g[here, cols].astype(F32) * att[here, cols] * r
            sums.append(carry[h] + jnp.sum(term.reshape(HEAD_DIM // 8, 8, HEAD_DIM), axis=0))
        return tuple(sums)

    zero = jnp.zeros((8, HEAD_DIM), F32)
    parts = lax.fori_loop(0, TOK // HEAD_DIM, gains, (zero,) * NH)
    for h in range(NH):
        gchip[pl.ds(h, 1), :] = jnp.sum(parts[h], axis=0, keepdims=True)
        gchip[pl.ds(h + NH, 1), :] = jnp.zeros((1, HEAD_DIM), F32)
    for d in (4, 3, 5, 2, 6, 1, 7):
        c = chip_at(0, d)
        remote(gchip, gz.at[zz], 8, (2 * c + core, tp)).start()
    gz[zz] = gchip[...]
    lax.fori_loop(0, SECOND_SPLIT, mixing_unit, 0)
    wait2 = scan_back(1, 4, False, wait1)
    wait_z = remote(gz.at[pl.ds(0, ZS - 1)], gz.at[pl.ds(0, ZS - 1)], 8, sibling)
    wait_z.wait_recv()
    gzs[...] = jnp.sum(gz[...], axis=0)
    for p in crossed + [(2 * chip_at(d, 0) + core, tp) for d in (2, 1, 3)] + [sibling]:
        remote(gzs, gy.at[2 * yy + core], 9, p).start()
    gy[2 * yy + core] = gzs[...]
    lax.fori_loop(SECOND_SPLIT, 2 * NH, mixing_unit, 0)
    swap = swap_half(1, 4, False, wait2)

    def finish(heads):
        for h in heads:
            cols = rows(h, HEAD_DIM)
            for b in range(2):
                both = pl.ds(b * BLK, BLK)
                after = pref[1, b, cols, :]
                kg_ref[both, cols] = (dot_nt(v[both, cols], after) + kga[both, cols]).astype(BF16)
                vg_ref[both, cols] = (dot_nn(k[both, cols], after) + vga[both, cols]).astype(BF16)

    finish(own_heads)
    wait_y = remote(gy.at[pl.ds(0, 2 * YS - 1)], gy.at[pl.ds(0, 2 * YS - 1)], 9, sibling)
    wait_y.wait_recv()
    gg_ref[...] = jnp.sum(gy[...], axis=0)[:NH]
    give.wait_send()
    wait1.wait_send()
    wait2.wait_send()
    wait_z.wait_send()
    wait_y.wait_send()
    swap.wait_recv()
    round_half(1, other, False)
    finish(other_heads)
    swap.wait_send()


def deliver(qg, kg, vg, gg, qg_hbm, kg_hbm, vg_hbm, gg_hbm, sem):
    copies = [
        pltpu.make_async_copy(src, dst, sem.at[i])
        for i, (src, dst) in enumerate(((qg, qg_hbm), (kg, kg_hbm), (vg, vg_hbm), (gg, gg_hbm)))
    ]
    for copy in copies:
        copy.start()
    for copy in copies:
        copy.wait()


def local(queries, keys, values, out_grad, gain):
    vmem = pltpu.VMEM
    big = jax.ShapeDtypeStruct((TOK, FEAT), BF16)
    state = (2, NH * HEAD_DIM, HEAD_DIM)
    half = (2, HALF, HEAD_DIM)
    tile = (8, HEAD_DIM)
    outside = pl.BlockSpec(memory_space=pltpu.HBM)
    whole = pl.BlockSpec(memory_space=vmem)
    results = (big, big, big, jax.ShapeDtypeStruct((NH, HEAD_DIM), F32))
    out = pl.pallas_call(
        kernel,
        name="attention_backward",
        out_shape=results,
        in_specs=[outside] * 5,
        out_specs=(whole,) * 4,
        scratch_shapes=[
            vmem((TOK, FEAT), BF16),
            vmem((TOK, FEAT), BF16),
            vmem((TOK, FEAT), BF16),
            vmem((TOK, FEAT), BF16),
            vmem((1, FEAT), F32),
            vmem((2 * NH, BLK, BLK), BF16),
            vmem((TOK, FEAT), F32),
            vmem((TOK, FEAT), F32),
            vmem((TOK, FEAT), BF16),
            vmem((TOK, FEAT), F32),
            vmem((TOK, FEAT), F32),
            vmem((TOK, HEAD_DIM), F32),
            vmem((TOK, HEAD_DIM), F32),
            vmem(state, F32),
            vmem(state, F32),
            vmem(half, F32),
            vmem(half, F32),
            vmem(half, F32),
            vmem(half, F32),
            vmem(half, F32),
            vmem(half, F32),
            vmem(state, F32),
            vmem((2,) + state, BF16),
            vmem((16, HEAD_DIM), F32),
            vmem((3, 16, HEAD_DIM), F32),
            vmem(tile, F32),
            vmem((ZS, 8, HEAD_DIM), F32),
            vmem(tile, F32),
            vmem((2 * YS, 8, HEAD_DIM), F32),
            pltpu.SemaphoreType.DMA((5,)),
            pltpu.SemaphoreType.DMA((14,)),
            pltpu.SemaphoreType.DMA((14,)),
        ],
        compiler_params=pltpu.CompilerParams(
            collective_id=0, has_side_effects=True, vmem_limit_bytes=53000000
        ),
    )(queries, keys, values, out_grad, gain.reshape(1, FEAT))
    out = pl.pallas_call(
        deliver,
        name="deliver",
        out_shape=results,
        in_specs=[whole] * 4,
        out_specs=(outside,) * 4,
        scratch_shapes=[pltpu.SemaphoreType.DMA((4,))],
        compiler_params=pltpu.CompilerParams(vmem_limit_bytes=1024 * 1024),
    )(*out)
    return out[0], out[1], out[2], out[3].reshape(FEAT)


def solution(mesh):
    in_specs = (P("seq", "tp"), P("seq", "tp"), P("seq", "tp"), P("seq", "tp"), P("tp"))
    out_specs = (P("seq", "tp"), P("seq", "tp"), P("seq", "tp"), P("tp"))
    return jax.shard_map(local, mesh=mesh, in_specs=in_specs, out_specs=out_specs, check_vma=False)
```

time: 56 us -> 50.1 us (0.89)
  local copies, waits for them, and re-layouts: 6.61 us -> 0.67 us
    unnamed x10 -> x2, local copies, waits for them, and re-layouts: 6.61 us -> 0.67 us
    pallas_call x1 -> x2, Pallas kernels: 48.5 us -> 48.7 us  [the longest x1 47 us: local(): pl.pallas_call(kernel, name='attention_backward', out_shape=results, in_s...]
where the time goes in v2:
time: 50.1 us; the launch traced here: 50 us
  Pallas kernels  48.7 us (97%)
  local copies, waits for them, and re-layouts  0.67 us (1%)
  between operations  0.65 us (1%)
    pallas_call x1, Pallas kernels, local(): pl.pallas_call(kernel, name='attention_backward', out_shape=results, in_s...  47 us
    pallas_call x1, Pallas kernels, local(): pl.pallas_call(deliver, name='deliver', out_shape=results, in_specs=[whol...  1.7 us

profile of v2, /device:TPU:1, one launch (start us, length us, event | category | flops | bytes accessed | tf_op | source)
XLA Modules:
  0.0 50.0 jit_solution(2315760941641772763)
XLA Ops:
  0.6 0.0 copy-start
  0.6 0.7 %copy-done = f32[512]{0:T(512)S(1)} copy-done((f32[512]{0:T(512)S(1)}, f32[512]{0:T(512)}, u32[]{:S(2)}) %copy-start) | copy-done | bytes 2072
  1.3 47.0 %attention_backward.1 = (bf16[1024,512]{1,0:T(8,128)(2,1)S(1)}, bf16[1024,512]{1,0:T(8,128)(2,1)S(1)}, bf16[1024,512]{1,0:T(8,128)(2,1)S(1)}, f32[4,128]{1,0:T(4,128)S(1)}) custom-call(bf16[1024,512]{1,0:T(8,128)(2,1)} %q_hbm.1, bf16[1024,512]{1,0:T(8,128)(2,1)} %k_hbm.1, bf16[1024,512]{1,0:T(8,128)(2,1)} %v_hbm.1, bf16[1024,512]{1,0:T(8,128)(2,1)} %g_hbm.1, ...), custom_call_target="tpu_custom_call" | custom-call | tf_op jit(solution)/shard_map/attention_backward/pallas_call | solution.py:365
  48.3 1.7 %deliver.1 = (bf16[1024,512]{1,0:T(8,128)(2,1)}, bf16[1024,512]{1,0:T(8,128)(2,1)}, bf16[1024,512]{1,0:T(8,128)(2,1)}, f32[4,128]{1,0:T(4,128)}) custom-call(bf16[1024,512]{1,0:T(8,128)(2,1)S(1)} %get-tuple-element.12.qg, bf16[1024,512]{1,0:T(8,128)(2,1)S(1)} %get-tuple-element.13.kg, bf16[1024,512]{1,0:T(8,128)(2,1)S(1)} %get-tuple-element.14.vg, ...), custom_call_target="tpu_custom_call" | custom-call | tf_op jit(solution)/shard_map/deliver/pallas_call | solution.py:409
Async XLA Ops:
  0.6 0.7 %copy-start = (f32[512]{0:T(512)S(1)}, f32[512]{0:T(512)}, u32[]{:S(2)}) copy-start(f32[512]{0:T(512)} %param.9) | copy-start | bytes 6148

commit v3 on v2

--- a/solution.py
+++ b/solution.py
@@ -23,7 +23,6 @@
 
 FIRST_SPLIT = 5
 SECOND_SPLIT = 4
-UNROLL = 8
 
 
 def ring(n, d):
@@ -50,10 +49,10 @@
 
 def kernel(
     q_hbm, k_hbm, v_hbm, g_hbm, gain_hbm,
-    qg_ref, kg_ref, vg_ref, gg_ref,
-    q, k, v, g, gain, sc, att, scaled, da, kga, vga, rcol, mcol,
+    qg_ref, kg_ref, vg_ref, gg_ref, k, v, kga, vga, after_ref,
+    q, g, gain, sc, att, scaled, da, rcol, mcol,
     inside, total, sib, piece, rb1, ob1, rb2, xb, edge, pref,
-    tpo, tpr, gchip, gz, gzs, gy,
+    tpo, tpr, coef, gchip, gz, gzs, gy,
     load_sem, send_sem, recv_sem,
 ):
     me = lax.axis_index("seq")
@@ -82,8 +81,8 @@
             ((k_hbm, k), (v_hbm, v), (q_hbm, q), (g_hbm, g), (gain_hbm, gain))
         )
     ]
-    for load in loads:
-        load.start()
+    loads[0].start()
+    loads[1].start()
 
     def remote(src, dst, index, device):
         return pltpu.make_async_remote_copy(
@@ -141,7 +140,7 @@
         top = jnp.where(causal, dot_nt(d_up, v[upper, cols]), 0.0).astype(BF16)
         low = dot_nt(d_low, v[upper, cols]).astype(BF16)
         end = jnp.where(causal, dot_nt(d_low, v[lower, cols]), 0.0).astype(BF16)
-        before = pref[0, b, cols, :]
+        before = pref[b, cols, :]
         k_up, k_low = k[upper, cols], k[lower, cols]
         qg_ref[upper, cols] = (dot_nt(d_up, before) + dot_nn(top, k_up)).astype(BF16)
         qg_ref[lower, cols] = (
@@ -191,8 +190,9 @@
     def round_half(scan, half, forward):
         reach = edge[scan, half, :]
         further = (reach + inside[scan, half, :]).astype(BF16)
-        pref[scan, 0 if forward else 1, half, :] = reach.astype(BF16)
-        pref[scan, 1 if forward else 0, half, :] = further
+        into = pref if forward else after_ref
+        into[0 if forward else 1, half, :] = reach.astype(BF16)
+        into[1 if forward else 0, half, :] = further
 
     def swap_half(scan, base, forward, wait2):
         wait2.wait_recv()
@@ -207,6 +207,8 @@
 
     loads[0].wait()
     loads[1].wait()
+    for load in loads[2:]:
+        load.start()
     states(other_heads + own_heads, k, v, 0, 0)
     pl.semaphore_wait(barrier, len(peers))
     give = give_half(0, 0)
@@ -219,57 +221,57 @@
     lax.fori_loop(FIRST_SPLIT, 2 * NH, score_unit, 0)
     swap = swap_half(0, 0, True, wait2)
 
-    def attend(heads, second):
-        def body(i, carry):
-            b = i // (BLK // HEAD_DIM)
-            here = rows(i, HEAD_DIM)
+    groups = BLK // HEAD_DIM
+
+    def attend(heads, second, b):
+        def body(j, carry):
+            here = rows(b * groups + j, HEAD_DIM)
             squares, inner = (rcol[here], mcol[here]) if second else (0.0, 0.0)
             for h in heads:
                 cols = rows(h, HEAD_DIM)
-                a = att[here, cols] + dot_nn(q[here, cols], pref[0, b, cols, :])
+                a = att[here, cols] + dot_nn(q[here, cols], pref[b, cols, :])
                 att[here, cols] = a
                 squares = squares + a * a
                 inner = inner + scaled[here, cols] * a
             if second:
                 sq = jnp.sum(squares, axis=1, keepdims=True)
                 inn = jnp.sum(inner, axis=1, keepdims=True)
-                tpo[pl.ds(i, 1), :] = jnp.sum(jnp.where(eye, sq, 0.0), axis=0, keepdims=True)
-                tpo[pl.ds(i + 8, 1), :] = jnp.sum(jnp.where(eye, inn, 0.0), axis=0, keepdims=True)
+                tpo[b, pl.ds(j, 1), :] = jnp.sum(jnp.where(eye, sq, 0.0), axis=0, keepdims=True)
+                tpo[b, pl.ds(j + groups, 1), :] = jnp.sum(
+                    jnp.where(eye, inn, 0.0), axis=0, keepdims=True
+                )
             else:
                 rcol[here] = squares
                 mcol[here] = inner
             return carry
 
-        lax.fori_loop(0, TOK // HEAD_DIM, body, 0, unroll=UNROLL)
-
-    attend(own_heads, False)
+        lax.fori_loop(0, groups, body, 0, unroll=True)
+
+    attend(own_heads, False, 0)
+    attend(own_heads, False, 1)
     swap.wait_recv()
     round_half(0, other, True)
-    attend(other_heads, True)
-    sends = [remote(tpo, tpr.at[i], 11 + i, t) for i, t in enumerate(tps)]
-    for s in sends:
-        s.start()
+    sends = []
+    for b in range(2):
+        attend(other_heads, True, b)
+        sends.append([remote(tpo.at[b], tpr.at[i, b], 11 + 3 * b + i, t) for i, t in enumerate(tps)])
+        for x in sends[b]:
+            x.start()
     give.wait_send()
     wait1.wait_send()
     wait2.wait_send()
     swap.wait_send()
-    for s in sends:
-        s.wait_recv()
-    sums = tpo[...] + tpr[0] + tpr[1] + tpr[2]
-    for s in sends:
-        s.wait_send()
-    inverse = lax.rsqrt(sums[:8] / FULL + EPS)
-    tpo[pl.ds(0, 8), :] = inverse
-    tpo[pl.ds(8, 8), :] = inverse * inverse * inverse * (sums[8:] / FULL)
-
-    def grads(heads, second):
-        def body(i, carry):
-            here = rows(i, HEAD_DIM)
+
+    def grads(heads, second, b):
+        def body(j, carry):
+            here = rows(b * groups + j, HEAD_DIM)
             if second:
                 r, m = rcol[here], mcol[here]
             else:
-                r = jnp.sum(jnp.where(eye, tpo[pl.ds(i, 1), :], 0.0), axis=1, keepdims=True)
-                m = jnp.sum(jnp.where(eye, tpo[pl.ds(i + 8, 1), :], 0.0), axis=1, keepdims=True)
+                r = jnp.sum(jnp.where(eye, coef[b, pl.ds(j, 1), :], 0.0), axis=1, keepdims=True)
+                m = jnp.sum(
+                    jnp.where(eye, coef[b, pl.ds(j + groups, 1), :], 0.0), axis=1, keepdims=True
+                )
                 r = jnp.broadcast_to(r, (HEAD_DIM, HEAD_DIM))
                 m = jnp.broadcast_to(m, (HEAD_DIM, HEAD_DIM))
                 rcol[here] = r
@@ -279,12 +281,20 @@
                 da[here, cols] = (r * scaled[here, cols] - m * att[here, cols]).astype(BF16)
             return carry
 
-        lax.fori_loop(0, TOK // HEAD_DIM, body, 0, unroll=UNROLL)
-
-    grads(other_heads, False)
+        lax.fori_loop(0, groups, body, 0, unroll=True)
+
+    for b in range(2):
+        for x in sends[b]:
+            x.wait_recv()
+        sums = tpo[b] + tpr[0, b] + tpr[1, b] + tpr[2, b]
+        inverse = lax.rsqrt(sums[:groups] / FULL + EPS)
+        coef[b, pl.ds(0, groups), :] = inverse
+        coef[b, pl.ds(groups, groups), :] = inverse * inverse * inverse * (sums[groups:] / FULL)
+        grads(other_heads, False, b)
     states(other_heads, q, da, 1, 1)
     give = give_half(1, 4)
-    grads(own_heads, True)
+    grads(own_heads, True, 0)
+    grads(own_heads, True, 1)
     states(own_heads, q, da, 1, 1)
     wait1 = spread(1, 4, give)
 
@@ -318,16 +328,13 @@
     lax.fori_loop(SECOND_SPLIT, 2 * NH, mixing_unit, 0)
     swap = swap_half(1, 4, False, wait2)
 
-    def finish(heads):
-        for h in heads:
-            cols = rows(h, HEAD_DIM)
-            for b in range(2):
-                both = pl.ds(b * BLK, BLK)
-                after = pref[1, b, cols, :]
-                kg_ref[both, cols] = (dot_nt(v[both, cols], after) + kga[both, cols]).astype(BF16)
-                vg_ref[both, cols] = (dot_nn(k[both, cols], after) + vga[both, cols]).astype(BF16)
-
-    finish(own_heads)
+    for n, h in enumerate(own_heads):
+        cols, to = rows(h, HEAD_DIM), pl.ds(n * HEAD_DIM, HEAD_DIM)
+        for b in range(2):
+            both = pl.ds(b * BLK, BLK)
+            after = after_ref[b, cols, :]
+            kg_ref[both, to] = (dot_nt(v[both, cols], after) + kga[both, cols]).astype(BF16)
+            vg_ref[both, to] = (dot_nn(k[both, cols], after) + vga[both, cols]).astype(BF16)
     wait_y = remote(gy.at[pl.ds(0, 2 * YS - 1)], gy.at[pl.ds(0, 2 * YS - 1)], 9, sibling)
     wait_y.wait_recv()
     gg_ref[...] = jnp.sum(gy[...], axis=0)[:NH]
@@ -336,19 +343,41 @@
     wait2.wait_send()
     wait_z.wait_send()
     wait_y.wait_send()
+    for x in sends[0] + sends[1]:
+        x.wait_send()
     swap.wait_recv()
     round_half(1, other, False)
-    finish(other_heads)
     swap.wait_send()
 
 
-def deliver(qg, kg, vg, gg, qg_hbm, kg_hbm, vg_hbm, gg_hbm, sem):
-    copies = [
-        pltpu.make_async_copy(src, dst, sem.at[i])
-        for i, (src, dst) in enumerate(((qg, qg_hbm), (kg, kg_hbm), (vg, vg_hbm), (gg, gg_hbm)))
-    ]
-    for copy in copies:
-        copy.start()
+def deliver(
+    qg, kg, vg, gg, k, v, kga, vga, after_ref,
+    qg_hbm, kg_hbm, vg_hbm, gg_hbm,
+    kgo, vgo, sem,
+):
+    core = lax.axis_index("seq") % 2
+    own = pl.ds(pl.multiple_of(core * HALF, HALF), HALF)
+    other = pl.ds(pl.multiple_of((1 - core) * HALF, HALF), HALF)
+    copies = []
+
+    def send(src, dst):
+        copies.append(pltpu.make_async_copy(src, dst, sem.at[len(copies)]))
+        copies[-1].start()
+
+    send(qg, qg_hbm)
+    send(kg, kg_hbm.at[:, own])
+    send(vg, vg_hbm.at[:, own])
+    send(gg, gg_hbm)
+    for b in range(2):
+        both = pl.ds(b * BLK, BLK)
+        for n in range(2):
+            cols = pl.ds(pl.multiple_of((2 - 2 * core + n) * HEAD_DIM, HEAD_DIM), HEAD_DIM)
+            to = pl.ds(n * HEAD_DIM, HEAD_DIM)
+            after = after_ref[b, cols, :]
+            kgo[both, to] = (dot_nt(v[both, cols], after) + kga[both, cols]).astype(BF16)
+            vgo[both, to] = (dot_nn(k[both, cols], after) + vga[both, cols]).astype(BF16)
+        send(kgo.at[both], kg_hbm.at[both, other])
+        send(vgo.at[both], vg_hbm.at[both, other])
     for copy in copies:
         copy.wait()
 
@@ -362,15 +391,19 @@
     outside = pl.BlockSpec(memory_space=pltpu.HBM)
     whole = pl.BlockSpec(memory_space=vmem)
     results = (big, big, big, jax.ShapeDtypeStruct((NH, HEAD_DIM), F32))
+    part = vmem((TOK, HALF), BF16)
+    entire = vmem((TOK, FEAT), BF16)
+    wide = vmem((TOK, FEAT), F32)
+    kept = (
+        entire, part, part, vmem((NH, HEAD_DIM), F32), entire, entire, wide, wide, vmem(state, BF16)
+    )
     out = pl.pallas_call(
         kernel,
         name="attention_backward",
-        out_shape=results,
+        out_shape=kept,
         in_specs=[outside] * 5,
-        out_specs=(whole,) * 4,
+        out_specs=(whole,) * len(kept),
         scratch_shapes=[
-            vmem((TOK, FEAT), BF16),
-            vmem((TOK, FEAT), BF16),
             vmem((TOK, FEAT), BF16),
             vmem((TOK, FEAT), BF16),
             vmem((1, FEAT), F32),
@@ -378,8 +411,6 @@
             vmem((TOK, FEAT), F32),
             vmem((TOK, FEAT), F32),
             vmem((TOK, FEAT), BF16),
-            vmem((TOK, FEAT), F32),
-            vmem((TOK, FEAT), F32),
             vmem((TOK, HEAD_DIM), F32),
             vmem((TOK, HEAD_DIM), F32),
             vmem(state, F32),
@@ -391,29 +422,33 @@
             vmem(half, F32),
             vmem(half, F32),
             vmem(state, F32),
-            vmem((2,) + state, BF16),
-            vmem((16, HEAD_DIM), F32),
-            vmem((3, 16, HEAD_DIM), F32),
+            vmem(state, BF16),
+            vmem((2,) + tile, F32),
+            vmem((3, 2) + tile, F32),
+            vmem((2,) + tile, F32),
             vmem(tile, F32),
             vmem((ZS, 8, HEAD_DIM), F32),
             vmem(tile, F32),
             vmem((2 * YS, 8, HEAD_DIM), F32),
             pltpu.SemaphoreType.DMA((5,)),
-            pltpu.SemaphoreType.DMA((14,)),
-            pltpu.SemaphoreType.DMA((14,)),
+            pltpu.SemaphoreType.DMA((17,)),
+            pltpu.SemaphoreType.DMA((17,)),
         ],
         compiler_params=pltpu.CompilerParams(
-            collective_id=0, has_side_effects=True, vmem_limit_bytes=53000000
+            collective_id=0, has_side_effects=True, vmem_limit_bytes=40 * 1024 * 1024
         ),
-    )(queries, keys, values, out_grad, gain.reshape(1, FEAT))
+    )(*(
+        pltpu.with_memory_space_constraint(x, pltpu.HBM)
+        for x in (queries, keys, values, out_grad, gain.reshape(1, FEAT))
+    ))
     out = pl.pallas_call(
         deliver,
         name="deliver",
         out_shape=results,
-        in_specs=[whole] * 4,
+        in_specs=[whole] * len(kept),
         out_specs=(outside,) * 4,
-        scratch_shapes=[pltpu.SemaphoreType.DMA((4,))],
-        compiler_params=pltpu.CompilerParams(vmem_limit_bytes=1024 * 1024),
+        scratch_shapes=[part, part, pltpu.SemaphoreType.DMA((8,))],
+        compiler_params=pltpu.CompilerParams(vmem_limit_bytes=20 * 1024 * 1024),
     )(*out)
     return out[0], out[1], out[2], out[3].reshape(FEAT)
 

time: 50.1 us -> 49.3 us (0.984)
  local copies, waits for them, and re-layouts: 0.67 us -> 0 us
    unnamed x2 -> x0, local copies, waits for them, and re-layouts: 0.67 us -> none
where the time goes in v3:
time: 49.3 us; the launch traced here: 49.2 us
  Pallas kernels  48.6 us (99%)
  between operations  0.64 us (1%)
    pallas_call x1, Pallas kernels, local(): pl.pallas_call(kernel, name='attention_backward', out_shape=kept, in_spec...  46.8 us
    pallas_call x1, Pallas kernels, local(): pl.pallas_call(deliver, name='deliver', out_shape=results, in_specs=[whol...  1.75 us

profile of v3, /device:TPU:1, one launch (start us, length us, event | category | flops | bytes accessed | tf_op | source)
XLA Modules:
  0.0 49.2 jit_solution(6380237592237956404)
XLA Ops:
  0.6 46.8 %attention_backward.1 = (bf16[1024,512]{1,0:T(8,128)(2,1)S(1)}, bf16[1024,256]{1,0:T(8,128)(2,1)S(1)}, bf16[1024,256]{1,0:T(8,128)(2,1)S(1)}, f32[4,128]{1,0:T(4...) custom-call(bf16[1024,512]{1,0:T(8,128)(2,1)} %q_hbm.1, ...), custom_call_target="tpu_custom_call" | custom-call | tf_op jit(solution)/shard_map/attention_backward/pallas_call | solution.py:400
  47.4 1.7 %deliver.1 = (bf16[1024,512]{1,0:T(8,128)(2,1)}, bf16[1024,512]{1,0:T(8,128)(2,1)}, bf16[1024,512]{1,0:T(8,128)(2,1)}, f32[4,128]{1,0:T(4,128)}) custom-call(bf16[1024,512]{1,0:T(8,128)(2,1)S(1)} %get-tuple-element.17.qg, bf16[1024,256]{1,0:T(8,128)(2,1)S(1)} %get-tuple-element.18.kg, bf16[1024,256]{1,0:T(8,128)(2,1)S(1)} %get-tuple-element.19.vg, ...), custom_call_target="tpu_custom_call" | custom-call | tf_op jit(solution)/shard_map/deliver/pallas_call | solution.py:444

commit v4 on v3

--- a/solution.py
+++ b/solution.py
@@ -66,7 +66,8 @@
     def chip_at(dy, dz):
         return (yy + dy) % YS * ZS + (zz + dz) % ZS
 
-    chips = [chip_at(dy, dz) for dy, dz in OFFSETS]
+    turn = 1 - 2 * core
+    chips = [chip_at(YS + turn * dy, ZS + turn * dz) for dy, dz in OFFSETS]
     crossed = [(2 * chip_at(dy, 0) + 1 - core, tp) for dy in (2, 1, 3)]
     tps = [(me, (tp + d) % 4) for d in (2, 1, 3)]
 
@@ -209,9 +210,10 @@
     loads[1].wait()
     for load in loads[2:]:
         load.start()
-    states(other_heads + own_heads, k, v, 0, 0)
+    states(other_heads, k, v, 0, 0)
     pl.semaphore_wait(barrier, len(peers))
     give = give_half(0, 0)
+    states(own_heads, k, v, 0, 0)
     loads[2].wait()
     loads[3].wait()
     loads[4].wait()

time: 49.3 us -> 49.3 us (level)
  no operation moved by 1% of the time
where the time goes in v4:
time: 49.3 us; the launch traced here: 49.2 us
  Pallas kernels  48.5 us (98%)
  between operations  0.64 us (1%)
    pallas_call x1, Pallas kernels, local(): pl.pallas_call(kernel, name='attention_backward', out_shape=kept, in_spec...  46.8 us
    pallas_call x1, Pallas kernels, local(): pl.pallas_call(deliver, name='deliver', out_shape=results, in_specs=[whol...  1.75 us

profile of v4, /device:TPU:1, one launch (start us, length us, event | category | flops | bytes accessed | tf_op | source)
XLA Modules:
  0.0 49.2 jit_solution(8381321176585504863)
XLA Ops:
  0.6 46.8 %attention_backward.1 = (bf16[1024,512]{1,0:T(8,128)(2,1)S(1)}, bf16[1024,256]{1,0:T(8,128)(2,1)S(1)}, bf16[1024,256]{1,0:T(8,128)(2,1)S(1)}, f32[4,128]{1,0:T(4...) custom-call(bf16[1024,512]{1,0:T(8,128)(2,1)} %q_hbm.1, ...), custom_call_target="tpu_custom_call" | custom-call | tf_op jit(solution)/shard_map/attention_backward/pallas_call | solution.py:402
  47.4 1.7 %deliver.1 = (bf16[1024,512]{1,0:T(8,128)(2,1)}, bf16[1024,512]{1,0:T(8,128)(2,1)}, bf16[1024,512]{1,0:T(8,128)(2,1)}, f32[4,128]{1,0:T(4,128)}) custom-call(bf16[1024,512]{1,0:T(8,128)(2,1)S(1)} %get-tuple-element.17.qg, bf16[1024,256]{1,0:T(8,128)(2,1)S(1)} %get-tuple-element.18.kg, bf16[1024,256]{1,0:T(8,128)(2,1)S(1)} %get-tuple-element.19.vg, ...), custom_call_target="tpu_custom_call" | custom-call | tf_op jit(solution)/shard_map/deliver/pallas_call | solution.py:446

commit v5 on v4

--- a/solution.py
+++ b/solution.py
@@ -314,7 +314,6 @@
     parts = lax.fori_loop(0, TOK // HEAD_DIM, gains, (zero,) * NH)
     for h in range(NH):
         gchip[pl.ds(h, 1), :] = jnp.sum(parts[h], axis=0, keepdims=True)
-        gchip[pl.ds(h + NH, 1), :] = jnp.zeros((1, HEAD_DIM), F32)
     for d in (4, 3, 5, 2, 6, 1, 7):
         c = chip_at(0, d)
         remote(gchip, gz.at[zz], 8, (2 * c + core, tp)).start()
@@ -339,7 +338,7 @@
             vg_ref[both, to] = (dot_nn(k[both, cols], after) + vga[both, cols]).astype(BF16)
     wait_y = remote(gy.at[pl.ds(0, 2 * YS - 1)], gy.at[pl.ds(0, 2 * YS - 1)], 9, sibling)
     wait_y.wait_recv()
-    gg_ref[...] = jnp.sum(gy[...], axis=0)[:NH]
+    gg_ref[...] = jnp.sum(gy[...], axis=0)
     give.wait_send()
     wait1.wait_send()
     wait2.wait_send()
@@ -428,10 +427,10 @@
             vmem((2,) + tile, F32),
             vmem((3, 2) + tile, F32),
             vmem((2,) + tile, F32),
-            vmem(tile, F32),
-            vmem((ZS, 8, HEAD_DIM), F32),
-            vmem(tile, F32),
-            vmem((2 * YS, 8, HEAD_DIM), F32),
+            vmem((NH, HEAD_DIM), F32),
+            vmem((ZS, NH, HEAD_DIM), F32),
+            vmem((NH, HEAD_DIM), F32),
+            vmem((2 * YS, NH, HEAD_DIM), F32),
             pltpu.SemaphoreType.DMA((5,)),
             pltpu.SemaphoreType.DMA((17,)),
             pltpu.SemaphoreType.DMA((17,)),

time: 49.3 us -> 49.3 us (level)
  no operation moved by 1% of the time
where the time goes in v5:
time: 49.3 us; the launch traced here: 49.2 us
  Pallas kernels  48.5 us (98%)
  between operations  0.64 us (1%)
    pallas_call x1, Pallas kernels, local(): pl.pallas_call(kernel, name='attention_backward', out_shape=kept, in_spec...  46.8 us
    pallas_call x1, Pallas kernels, local(): pl.pallas_call(deliver, name='deliver', out_shape=results, in_specs=[whol...  1.75 us

profile of v5, /device:TPU:1, one launch (start us, length us, event | category | flops | bytes accessed | tf_op | source)
XLA Modules:
  0.0 49.2 jit_solution(17577618435738923697)
XLA Ops:
  0.6 46.8 %attention_backward.1 = (bf16[1024,512]{1,0:T(8,128)(2,1)S(1)}, bf16[1024,256]{1,0:T(8,128)(2,1)S(1)}, bf16[1024,256]{1,0:T(8,128)(2,1)S(1)}, f32[4,128]{1,0:T(4...) custom-call(bf16[1024,512]{1,0:T(8,128)(2,1)} %q_hbm.1, ...), custom_call_target="tpu_custom_call" | custom-call | tf_op jit(solution)/shard_map/attention_backward/pallas_call | solution.py:401
  47.4 1.7 %deliver.1 = (bf16[1024,512]{1,0:T(8,128)(2,1)}, bf16[1024,512]{1,0:T(8,128)(2,1)}, bf16[1024,512]{1,0:T(8,128)(2,1)}, f32[4,128]{1,0:T(4,128)}) custom-call(bf16[1024,512]{1,0:T(8,128)(2,1)S(1)} %get-tuple-element.17.qg, bf16[1024,256]{1,0:T(8,128)(2,1)S(1)} %get-tuple-element.18.kg, bf16[1024,256]{1,0:T(8,128)(2,1)S(1)} %get-tuple-element.19.vg, ...), custom_call_target="tpu_custom_call" | custom-call | tf_op jit(solution)/shard_map/deliver/pallas_call | solution.py:445
